TPU v7x, 32 devices: a whole 2x2x4 slice. The times are simulated.
32 devices in a mesh: ty: 4 (over y, core), tx: 8 (over z, x).
Axes of the slice: x: 2, y: 2, z: 4, core: 2. Of those that a mesh axis runs over, the one named last changes fastest.
Arguments:
- section_a: bfloat16 [2048, 4096], P('ty', 'tx'), may hold values from -6 to 6
- section_b: bfloat16 [2048, 4096], P('ty', 'tx'), may hold values from -6 to 6
- template_corner: int32 [2, 4, 64], P(None, 'ty', 'tx'), may hold values from 0 to 384
- template_slot: int32 [4, 64], P('ty', 'tx'), may hold values from 0 to 15, as said below
- window_corner: int32 [2, 4, 64], P(None, 'ty', 'tx'), may hold values from 0 to 384
- window_slot: int32 [4, 64], P('ty', 'tx'), may hold values from 0 to 15, as said below
- node_mask: int32 [128, 256], P('ty', 'tx'), may hold values 0 or 1
Outputs:
- owner_flow: float32 [2, 4, 64], P(None, 'ty', 'tx')
- source_flow: float32 [2, 4, 64], P(None, 'ty', 'tx')
- displacement: float32 [2, 128, 256], P(None, 'ty', 'tx')
Inputs may be any that keep to these rules, and one draw needn't show every extreme that they name: `template_slot`: entry j of a row belongs to owner device j // 8 of that ty row; its value is s * 2 + k for the k-th pair that source device s sends to it; the values of one device's list are distinct; each owner gets exactly 2 pairs from each of 4 sources. `window_slot`: entry m of a row belongs to source device m // 8 of that ty row; its value is o * 2 + k for the k-th pair that it sends to owner device o; the values of one device's list are distinct; together with template_slot every pair of a row appears once on each side.
All inputs are finite; a program needn't handle non-finite values. No bound on the sum of `node_mask` on one device may be relied on, other than what follows from the above.
Results may differ from a plain program's by a relative error of at most 0.0003.
Values may be sent and summed in bfloat16 or wider, within the bound.
A program may use at most 64 MiB of HBM per device.

v0:
```python
import functools

import jax
import jax.numpy as jnp
from jax import lax
from jax.experimental import pallas as pl
from jax.experimental.pallas import tpu as pltpu
from jax.sharding import PartitionSpec as P

PATCH = 128
SHIFTS = 65
RADIUS = 32
WIN = 192
CAP = 2
ITERS_R = 3
LANES = 128
GROUP = 4
SPAN = 128


SHARPNESS = 256.0
SPRING_RATE = 0.25
FLOW_RATE = 0.5
FLOW_UNIT = 8.0
EPSILON = 1e-05
VMEM = pl.BlockSpec(memory_space=pltpu.VMEM)
SMEM = pl.BlockSpec(memory_space=pltpu.SMEM)
ANY = pl.BlockSpec(memory_space=pl.ANY)


DIRECTIONS = tuple((r, c) for r in (-1, 0, 1) for c in (-1, 0, 1) if (r, c) != (0, 0))
MESH = pl.DeviceIdType.MESH


def within(n_ty, n_tx, row, col):
    return (row >= 0) & (row < n_ty) & (col >= 0) & (col < n_tx)


def greet(n_ty, n_tx):
    ty, tx = lax.axis_index("ty"), lax.axis_index("tx")
    barrier = pltpu.get_barrier_semaphore()
    waits = n_tx - 1
    for step in range(1, n_tx):
        pl.semaphore_signal(
            barrier, inc=1, device_id=(ty, lax.rem(tx + step, n_tx)), device_id_type=MESH
        )
    for r, c in DIRECTIONS:
        if r == 0:
            continue
        there = within(n_ty, n_tx, ty + r, tx + c)

        @pl.when(there)
        def _():
            pl.semaphore_signal(barrier, inc=1, device_id=(ty + r, tx + c), device_id_type=MESH)

        waits = waits + there.astype(jnp.int32)
    pl.semaphore_wait(barrier, waits)


def to_row(n_tx, source, landing, width, send, recv):
    ty, tx = lax.axis_index("ty"), lax.axis_index("tx")
    copies = []
    for step in range(1, n_tx):
        peer = lax.rem(tx + step, n_tx)
        copies.append(
            pltpu.make_async_remote_copy(
                src_ref=source.at[pl.ds(peer * width, width)],
                dst_ref=landing.at[pl.ds(tx * width, width)],
                send_sem=send.at[step],
                recv_sem=recv.at[step],
                device_id=(ty, peer),
                device_id_type=MESH,
            )
        )
    return copies


def edges_of(step, size, rim, pad):
    if step == 0:
        return pl.ds(0, size), pl.ds(pad, size)
    if step < 0:
        return pl.ds(0, rim), pl.ds(pad + size, rim)
    return pl.ds(size - rim, rim), pl.ds(pad - rim, rim)


def gather_kernel(n_ty, n_tx, b_ref, out_ref, wide, landed, zeros, send, recv, hsend, hrecv, own):
    ty, tx = lax.axis_index("ty"), lax.axis_index("tx")
    rows, cols = b_ref.shape
    zeros[...] = jnp.zeros(zeros.shape, zeros.dtype)
    tile_copy = pltpu.make_async_copy(
        b_ref, wide.at[pl.ds(RADIUS, rows), pl.ds(LANES, cols)], own.at[8]
    )
    tile_copy.start()
    mine = pl.ds(tx * CAP, CAP)
    own_copy = pltpu.make_async_copy(out_ref.at[mine], landed.at[mine], own.at[9])
    own_copy.start()
    greet(n_ty, n_tx)
    copies = to_row(n_tx, out_ref, landed, CAP, send, recv)
    for copy in copies:
        copy.start()
    rims = []
    for d, (r, c) in enumerate(DIRECTIONS):
        row_from, row_to = edges_of(r, rows, RADIUS, RADIUS)
        col_from, col_to = edges_of(c, cols, LANES, LANES)
        rim = pltpu.make_async_remote_copy(
            src_ref=b_ref.at[row_from, col_from],
            dst_ref=wide.at[row_to, col_to],
            send_sem=hsend.at[d],
            recv_sem=hrecv.at[d],
            device_id=(ty + r, tx + c),
            device_id_type=MESH,
        )
        fill = pltpu.make_async_copy(
            zeros.at[pl.ds(0, row_to.size), pl.ds(0, col_to.size)],
            wide.at[row_to, col_to],
            own.at[d],
        )
        goes = within(n_ty, n_tx, ty + r, tx + c)
        comes = within(n_ty, n_tx, ty - r, tx - c)
        pl.when(goes)(rim.start)
        pl.when(jnp.logical_not(comes))(fill.start)
        rims.append((goes, comes, rim, fill))
    for goes, comes, rim, fill in rims:
        pl.when(comes)(rim.wait_recv)
        pl.when(jnp.logical_not(comes))(fill.wait)
        pl.when(goes)(rim.wait_send)
    tile_copy.wait()
    own_copy.wait()
    for copy in copies:
        copy.wait()


def gather(section_b, outgoing, n_ty, n_tx):
    rows, cols = section_b.shape
    dma = pltpu.SemaphoreType.DMA
    return pl.pallas_call(
        functools.partial(gather_kernel, n_ty, n_tx),
        out_shape=[
            jax.ShapeDtypeStruct((rows + 2 * RADIUS, cols + 2 * LANES), jnp.bfloat16),
            jax.ShapeDtypeStruct(outgoing.shape, jnp.bfloat16),
        ],
        in_specs=[ANY, ANY],
        out_specs=[ANY, ANY],
        scratch_shapes=[
            pltpu.VMEM((rows, cols), jnp.bfloat16),
            dma((n_tx,)),
            dma((n_tx,)),
            dma((8,)),
            dma((8,)),
            dma((10,)),
        ],
        compiler_params=pltpu.CompilerParams(
            collective_id=0, has_side_effects=True, vmem_limit_bytes=8 * 2**20
        ),
        name="gather",
    )(section_b, outgoing)


def relax_kernel(
    n_ty, n_tx, slot_ref, ret_ref, field_ref, owner_ref, moved_ref, landed, ext, send, recv, hsend, hrecv
):
    f32 = jnp.float32
    ty, tx = lax.axis_index("ty"), lax.axis_index("tx")
    rows = field_ref.shape[0]
    cols = moved_ref.shape[2]
    items = owner_ref.shape[2]
    greet(n_ty, n_tx)
    copies = to_row(n_tx, ret_ref, landed, 1, send, recv)
    rims = []
    for d, (r, c) in enumerate(DIRECTIONS):
        row_from, row_to = edges_of(r, rows, 8, 8)
        rim = pltpu.make_async_remote_copy(
            src_ref=field_ref.at[row_from],
            dst_ref=ext.at[1 - c, row_to],
            send_sem=hsend.at[d],
            recv_sem=hrecv.at[d],
            device_id=(ty + r, tx + c),
            device_id_type=MESH,
        )
        goes = within(n_ty, n_tx, ty + r, tx + c)
        comes = within(n_ty, n_tx, ty - r, tx - c)
        pl.when(goes)(rim.start)
        rims.append((goes, comes, rim, 1 - c, row_to))
    for copy in copies:
        copy.start()
    landed[pl.ds(tx, 1)] = ret_ref[pl.ds(tx, 1)]
    ext[1, 8 : 8 + rows, :] = field_ref[...]
    for goes, comes, rim, side, row_to in rims:

        @pl.when(jnp.logical_not(comes))
        def _():
            ext[side, row_to, :] = jnp.zeros((row_to.size, LANES), f32)

    for goes, comes, rim, side, row_to in rims:
        pl.when(comes)(rim.wait_recv)
    lane = lax.broadcasted_iota(jnp.int32, (rows + 16, LANES), 1)
    left, middle, right = ext[0], ext[1], ext[2]

    def spread(field):
        at = field * cols
        wide = jnp.where(lane < 8 + cols, pltpu.roll(middle, (8 - at) % LANES, 1), 0.0)
        wide = jnp.where(lane < 8, pltpu.roll(left, (8 - at - cols) % LANES, 1), wide)
        beyond = (lane >= 8 + cols) & (lane < 16 + cols)
        return jnp.where(beyond, pltpu.roll(right, (8 + cols - at) % LANES, 1), wide)

    def around(grid):
        return (
            pltpu.roll(grid, 1, 0),
            pltpu.roll(grid, rows + 15, 0),
            pltpu.roll(grid, 1, 1),
            pltpu.roll(grid, LANES - 1, 1),
        )

    mask, count = spread(0), spread(3)
    pairs = [mask * near for near in around(mask)]
    for axis in range(2):
        target = spread(1 + axis)
        displace = jnp.zeros((rows + 16, LANES), f32)
        for sweep in range(ITERS_R):
            spring = jnp.zeros((rows + 16, LANES), f32)
            for pair, near in zip(pairs, around(displace)):
                spring = spring + pair * (near - displace)
            displace = (
                displace + SPRING_RATE * spring + FLOW_RATE * (target - count * displace)
            )
        moved_ref[axis] = pltpu.roll(displace, LANES - 8, 1)[8 : 8 + rows, :cols]
    for copy in copies:
        copy.wait()
    for goes, comes, rim, side, row_to in rims:
        pl.when(goes)(rim.wait_send)
    out_lane = lax.broadcasted_iota(jnp.int32, (1, LANES), 1)
    for axis in range(2):
        out = jnp.zeros((1, LANES), f32)
        for j in range(items):
            slot = slot_ref[0, j]
            value = landed[slot // CAP, pl.ds(slot % CAP * 2 + axis, 1), :]
            out = jnp.where(out_lane == j, value, out)
        owner_ref[axis] = out[:, :items]


def relax(template_slot, returned, field, cols, n_ty, n_tx):
    f32 = jnp.float32
    rows = field.shape[0]
    dma = pltpu.SemaphoreType.DMA
    return pl.pallas_call(
        functools.partial(relax_kernel, n_ty, n_tx),
        out_shape=[
            jax.ShapeDtypeStruct((2, 1, template_slot.shape[1]), f32),
            jax.ShapeDtypeStruct((2, rows, cols), f32),
        ],
        in_specs=[SMEM, VMEM, VMEM],
        out_specs=[VMEM, VMEM],
        scratch_shapes=[
            pltpu.VMEM(returned.shape, f32),
            pltpu.VMEM((3, rows + 16, LANES), f32),
            dma((n_tx,)),
            dma((n_tx,)),
            dma((8,)),
            dma((8,)),
        ],
        compiler_params=pltpu.CompilerParams(
            collective_id=1, has_side_effects=True, vmem_limit_bytes=8 * 2**20
        ),
        name="relax",
    )(template_slot, returned, field)


def cut_kernel(items, corner_ref, slot_ref, a_ref, out_ref, wide):
    rows, cols = a_ref.shape
    for part in range(cols // LANES):
        wide[part] = a_ref[:, part * LANES : (part + 1) * LANES].astype(jnp.float32)
    wide[cols // LANES] = jnp.zeros((rows, LANES), jnp.float32)

    def one(j, carry):
        top = corner_ref[0, 0, j]
        left = corner_ref[1, 0, j]
        base = left // LANES
        block = jnp.concatenate([wide[base + p, pl.ds(top, PATCH), :] for p in range(2)], axis=1)
        block = pltpu.roll(block, (2 * LANES - left % LANES) % (2 * LANES), 1)
        out_ref[slot_ref[0, j]] = block[:, :PATCH].astype(jnp.bfloat16)
        return carry

    lax.fori_loop(0, items, one, 0)


def cut_templates(section_a, template_corner, template_slot, slots):
    rows, cols = section_a.shape
    return pl.pallas_call(
        functools.partial(cut_kernel, template_slot.shape[1]),
        out_shape=jax.ShapeDtypeStruct((slots, PATCH, PATCH), jnp.bfloat16),
        in_specs=[SMEM, SMEM, VMEM],
        out_specs=VMEM,
        scratch_shapes=[pltpu.VMEM((cols // LANES + 1, rows, LANES), jnp.float32)],
        compiler_params=pltpu.CompilerParams(vmem_limit_bytes=24 * 2**20),
        name="cut",
    )(template_corner, template_slot, section_a)


def flow_kernel(
    items,
    left_pad,
    tile,
    corner_ref,
    slot_ref,
    b_ref,
    t_ref,
    mask_ref,
    ret_ref,
    field_ref,
    source_ref,
    wide,
    win,
    shifted,
    temp,
    corrs,
    scales,
):
    f32 = jnp.float32
    rows_b, cols_b = b_ref.shape
    for part in range(wide.shape[0]):
        held = max(0, min(LANES, cols_b - part * LANES))
        if held < LANES:
            wide[part] = jnp.zeros((rows_b, LANES), f32)
        if held:
            wide[part, :, :held] = b_ref[:, part * LANES : part * LANES + held].astype(f32)
    win[:, WIN:, :] = jnp.zeros((items, win.shape[1] - WIN, 2 * LANES), f32)
    lane = lax.broadcasted_iota(jnp.int32, (64, LANES), 1)
    shift = lax.broadcasted_iota(jnp.int32, (64, LANES), 0)
    low = (lane >= shift).astype(f32).astype(jnp.bfloat16)
    high = (lane < shift).astype(f32).astype(jnp.bfloat16)
    row_of = lax.broadcasted_iota(jnp.int32, (8, 2 * LANES), 0)
    win_lane = lax.broadcasted_iota(jnp.int32, (WIN, 2 * LANES), 1)

    def one(m, carry):
        top = corner_ref[0, 0, m]
        left = corner_ref[1, 0, m] + left_pad
        base = left // LANES
        block = jnp.concatenate([wide[base + p, pl.ds(top, WIN), :] for p in range(3)], axis=1)
        block = pltpu.roll(block, (3 * LANES - left % LANES) % (3 * LANES), 1)
        window = jnp.where(win_lane < WIN, block[:, : 2 * LANES], 0.0)
        win[m, :WIN, :] = window
        template = t_ref[slot_ref[0, m]]
        temp[m] = template.astype(f32)
        for s in range(16 // GROUP):
            shifted[m, s] = win[m, pl.ds(s * GROUP, shifted.shape[2]), :].astype(jnp.bfloat16)
        temp_f = temp[m]
        energy_t = jnp.sum(temp_f * temp_f, keepdims=True) / (PATCH * PATCH)
        energy_w = jnp.sum(window * window, keepdims=True) / (WIN * WIN)
        scales[m] = jnp.broadcast_to((energy_t + EPSILON) * (energy_w + EPSILON), (8, LANES))

        def rows16(step, total):
            row0 = pl.multiple_of(step * 16, 16)
            sixteen = temp[m, pl.ds(row0, 16), :]
            placed, moved = [], []
            for s in range(16 // GROUP):
                parts = []
                for g in range(GROUP):
                    row = jnp.broadcast_to(
                        sixteen[s * GROUP + g : s * GROUP + g + 1, :], (64, LANES)
                    )
                    turned = pltpu.roll(row, 0, 1, stride=1, stride_axis=0)
                    turned = turned.astype(jnp.bfloat16)
                    parts.append(jnp.concatenate([turned * low, turned * high], axis=1))
                placed.append(jnp.concatenate(parts, axis=0))
                moved.append(shifted[m, s, pl.ds(row0, SPAN), :])
            return total + lax.dot_general(
                jnp.concatenate(placed, axis=1),
                jnp.concatenate(moved, axis=1),
                (((1,), (1,)), ((), ())),
                preferred_element_type=f32,
            )

        total = lax.fori_loop(
            0, PATCH // 16, rows16, jnp.zeros((GROUP * 64, SPAN), f32), unroll=True
        )
        corr = total[:64]
        for g in range(1, GROUP):
            corr = corr + pltpu.roll(total[g * 64 : g * 64 + 64], SPAN - g, 1)
        corrs[m, :64, :] = corr
        far = pltpu.roll(window, 2 * LANES - 64, 1)[:, :LANES].astype(jnp.bfloat16)
        far = jnp.concatenate([far, jnp.zeros((2 * LANES - WIN, LANES), jnp.bfloat16)], axis=0)
        cross = lax.dot_general(
            template, far, (((1,), (1,)), ((), ())), preferred_element_type=f32
        )
        moved = cross[:8]
        for q in range(1, PATCH // 8):
            moved = moved + pltpu.roll(cross[8 * q : 8 * q + 8], 2 * LANES - 8 * q, 1)
        for bit in (1, 2, 4):
            moved = jnp.where(row_of & bit != 0, pltpu.roll(moved, 2 * LANES - bit, 1), moved)
        last = jnp.sum(moved, axis=0, keepdims=True)
        corrs[m, 64:72, :] = jnp.broadcast_to(last[:, :LANES], (8, LANES))
        return carry

    lax.fori_loop(0, items, one, 0, unroll=4)

    corr = corrs[...]
    scale = SHARPNESS / (PATCH * PATCH * jnp.sqrt(scales[...]))
    dx = lax.broadcasted_iota(jnp.int32, corr.shape, 1)
    dy = lax.broadcasted_iota(jnp.int32, corr.shape, 2)
    inside = (dy < SHIFTS) & (dx < SHIFTS)
    scores = jnp.where(inside, corr * scale[:, 0:1, :], jnp.finfo(f32).min)
    peak = jnp.max(jnp.max(scores, axis=1, keepdims=True), axis=2, keepdims=True)
    weights = jnp.where(inside, jnp.exp(scores - peak), 0.0)
    by_col = jnp.sum(weights, axis=1, keepdims=True)
    norm = jnp.sum(by_col, axis=2, keepdims=True)
    dy_of = (dy[:, 0:1, :] - RADIUS).astype(f32)
    flow_y = jnp.sum(by_col * dy_of, axis=2, keepdims=True) / norm / FLOW_UNIT
    by_dx = jnp.sum(weights * (dx - RADIUS).astype(f32), axis=1, keepdims=True)
    flow_x = jnp.sum(by_dx, axis=2, keepdims=True) / norm / FLOW_UNIT
    flow_y = jnp.broadcast_to(flow_y, (items, 1, LANES))
    flow_x = jnp.broadcast_to(flow_x, (items, 1, LANES))
    node_rows, node_cols = mask_ref.shape
    at_row = lax.broadcasted_iota(jnp.int32, (node_rows, LANES), 0)
    at_col = lax.broadcasted_iota(jnp.int32, (node_rows, LANES), 1)
    field = jnp.zeros((node_rows, LANES), f32)
    out_lane = lax.broadcasted_iota(jnp.int32, (1, LANES), 1)
    out_y = jnp.zeros((1, LANES), f32)
    out_x = jnp.zeros((1, LANES), f32)
    for m in range(items):
        slot = slot_ref[0, m]
        ret_ref[slot // CAP, pl.ds(slot % CAP * 2, 1), :] = flow_y[m]
        ret_ref[slot // CAP, pl.ds(slot % CAP * 2 + 1, 1), :] = flow_x[m]
        centre_y = (corner_ref[0, 0, m] + PATCH // 2) * node_rows // tile
        centre_x = (corner_ref[1, 0, m] + PATCH // 2) * node_cols // tile
        here = at_row == centre_y
        for part, value in ((1, -flow_y[m]), (2, -flow_x[m]), (3, 1.0)):
            at = at_col == centre_x + part * node_cols
            field = field + jnp.where(here & at, value, 0.0)
        out_y = jnp.where(out_lane == m, -flow_y[m], out_y)
        out_x = jnp.where(out_lane == m, -flow_x[m], out_x)
    field_ref[...] = field
    field_ref[:, :node_cols] = mask_ref[...].astype(f32)
    source_ref[0] = out_y[:, :items]
    source_ref[1] = out_x[:, :items]


def pair_flows(wide_b, arrived, window_corner, window_slot, node_mask, left_pad, tile, devices):
    items = window_slot.shape[1]
    rows_b = wide_b.shape[0]
    node_rows = node_mask.shape[0]
    f32 = jnp.float32
    cols_w = max(wide_b.shape[1], (tile - PATCH + left_pad) // LANES * LANES + 3 * LANES)
    cols_w = (cols_w + LANES - 1) // LANES * LANES
    return pl.pallas_call(
        functools.partial(flow_kernel, items, left_pad, tile),
        out_shape=[
            jax.ShapeDtypeStruct((devices, 8, LANES), f32),
            jax.ShapeDtypeStruct((node_rows, LANES), f32),
            jax.ShapeDtypeStruct((2, 1, items), f32),
        ],
        in_specs=[SMEM, SMEM, VMEM, VMEM, VMEM],
        out_specs=[VMEM, VMEM, VMEM],
        scratch_shapes=[
            pltpu.VMEM((cols_w // LANES, rows_b, LANES), f32),
            pltpu.VMEM((items, WIN + 80, 2 * LANES), f32),
            pltpu.VMEM((items, 16 // GROUP, WIN + 64, 2 * LANES), jnp.bfloat16),
            pltpu.VMEM((items, PATCH, LANES), f32),
            pltpu.VMEM((items, 72, LANES), f32),
            pltpu.VMEM((items, 8, LANES), f32),
        ],
        compiler_params=pltpu.CompilerParams(vmem_limit_bytes=32 * 2**20),
        name="pair_flows",
    )(window_corner, window_slot, wide_b, arrived, node_mask)


def shards(
    section_a, section_b, template_corner, template_slot, window_corner, window_slot, node_mask
):
    tile = section_a.shape[0]
    n_ty, n_tx = lax.axis_size("ty"), lax.axis_size("tx")
    outgoing = cut_templates(section_a, template_corner, template_slot, n_tx * CAP)
    b_wide, arrived = gather(section_b, outgoing, n_ty, n_tx)
    returned, field, source_flow = pair_flows(
        b_wide, arrived, window_corner, window_slot, node_mask, LANES - RADIUS, tile, n_tx
    )
    owner_flow, displace = relax(
        template_slot, returned, field, node_mask.shape[1], n_ty, n_tx
    )
    return (owner_flow, source_flow, displace)


def solution(mesh):
    placed = (
        P("ty", "tx"),
        P("ty", "tx"),
        P(None, "ty", "tx"),
        P("ty", "tx"),
        P(None, "ty", "tx"),
        P("ty", "tx"),
        P("ty", "tx"),
    )
    return jax.shard_map(
        shards,
        mesh=mesh,
        in_specs=placed,
        out_specs=(P(None, "ty", "tx"), P(None, "ty", "tx"), P(None, "ty", "tx")),
        check_vma=False,
    )
```

profile of v0, /device:TPU:0, one launch (start us, length us, event | category | flops | bytes accessed | tf_op | source)
XLA Modules:
  0.0 48.0 jit_solution(4069163764251899112)
XLA Ops:
  0.6 0.0 copy-start
  0.6 1.0 %copy-done = bf16[512,512]{1,0:T(8,128)(2,1)S(1)} copy-done((bf16[512,512]{1,0:T(8,128)(2,1)S(1)}, bf16[512,512]{1,0:T(8,128)(2,1)}, u32[]{:S(2)}) %copy-start) | copy-done | bytes 524312
  1.7 0.0 copy-start.3
  1.7 0.7 %copy-done.3 = s32[1,8]{1,0:T(1,128)S(1)} copy-done((s32[1,8]{1,0:T(1,128)S(1)}, s32[1,8]{1,0:T(1,128)}, u32[]{:S(2)}) %copy-start.3) | copy-done | bytes 56
  2.3 0.0 copy-start.5
  2.3 0.7 %copy-done.5 = s32[2,1,8]{2,1,0:T(1,128)S(1)} copy-done((s32[2,1,8]{2,1,0:T(1,128)S(1)}, s32[2,1,8]{2,1,0:T(1,128)}, u32[]{:S(2)}) %copy-start.5) | copy-done | bytes 88
  3.0 0.0 copy-start.1
  3.0 1.4 %cut.1.out_ref = bf16[16,128,128]{2,1,0:T(8,128)(2,1)S(1)} custom-call(s32[2,1,8]{2,1,0:T(1,128)S(1)} %copy-done.5, s32[1,8]{1,0:T(1,128)S(1)} %copy-done.3, bf16[512,512]{1,0:T(8,128)(2,1)S(1)} %copy-done), custom_call_target="tpu_custom_call" | custom-call | tf_op jit(solution)/shard_map/cut/pallas_call | solution.py:288
  4.4 0.0 copy-done.1
  4.5 0.0 copy-start.2
  4.5 18.3 %gather.1 = (bf16[576,768]{1,0:T(8,128)(2,1)S(1)}, bf16[16,128,128]{2,1,0:T(8,128)(2,1)S(1)}) custom-call(bf16[512,512]{1,0:T(8,128)(2,1)S(1)} %copy-done.1, bf16[16,128,128]{2,1,0:T(8,128)(2,1)S(1)} %cut.1.out_ref), custom_call_target="tpu_custom_call" | custom-call | tf_op jit(solution)/shard_map/gather/pallas_call | solution.py:136
  22.8 0.0 copy-start.6
  22.8 0.0 copy-start.7
  22.8 0.0 copy-done.2
  22.8 0.6 %copy-done.6 = s32[2,1,8]{2,1,0:T(1,128)S(1)} copy-done((s32[2,1,8]{2,1,0:T(1,128)S(1)}, s32[2,1,8]{2,1,0:T(1,128)}, u32[]{:S(2)}) %copy-start.6) | copy-done | bytes 88
  23.4 0.0 copy-done.7
  23.4 12.0 %pair_flows.1 = (f32[8,8,128]{2,1,0:T(8,128)S(1)}, f32[32,128]{1,0:T(8,128)S(1)}, f32[2,1,8]{2,1,0:T(1,128)}) custom-call(s32[2,1,8]{2,1,0:T(1,128)S(1)} %copy-done.6, s32[1,8]{1,0:T(1,128)S(1)} %copy-done.7, bf16[576,768]{1,0:T(8,128)(2,1)S(1)} %get-tuple-element.10.b_ref, bf16[16,128,128]{2,1,0:T(8,128)(2,1)S(1)} %get-tuple-element.11.t_ref, ...), custom_call_target="tpu_custom_call" | custom-call | tf_op jit(solution)/shard_map/pair_flows/pallas_call | solution.py:444
  35.5 0.0 copy-start.4
  35.5 0.7 %copy-done.4 = s32[1,8]{1,0:T(1,128)S(1)} copy-done((s32[1,8]{1,0:T(1,128)S(1)}, s32[1,8]{1,0:T(1,128)}, u32[]{:S(2)}) %copy-start.4) | copy-done | bytes 56
  36.1 10.7 %relax.1 = (f32[2,1,8]{2,1,0:T(1,128)S(1)}, f32[2,32,32]{2,1,0:T(8,128)S(1)}) custom-call(s32[1,8]{1,0:T(1,128)S(1)} %copy-done.4, f32[8,8,128]{2,1,0:T(8,128)S(1)} %get-tuple-element.12.ret_ref, f32[32,128]{1,0:T(8,128)S(1)} %get-tuple-element.13.field_ref), custom_call_target="tpu_custom_call" | custom-call | tf_op jit(solution)/shard_map/relax/pallas_call | solution.py:245
  46.8 0.6 %copy.12 = f32[2,1,8]{2,1,0:T(1,128)} copy(f32[2,1,8]{2,1,0:T(1,128)S(1)} %get-tuple-element.20) | data formatting | bytes 128
  47.3 0.6 %copy.13 = f32[2,32,32]{2,1,0:T(8,128)} copy(f32[2,32,32]{2,1,0:T(8,128)S(1)} %get-tuple-element.22) | data formatting | bytes 16384
Async XLA Ops:
  0.6 1.0 %copy-start = (bf16[512,512]{1,0:T(8,128)(2,1)S(1)}, bf16[512,512]{1,0:T(8,128)(2,1)}, u32[]{:S(2)}) copy-start(bf16[512,512]{1,0:T(8,128)(2,1)} %a_ref.1) | copy-start | bytes 1572868
  1.7 0.7 %copy-start.3 = (s32[1,8]{1,0:T(1,128)S(1)}, s32[1,8]{1,0:T(1,128)}, u32[]{:S(2)}) copy-start(s32[1,8]{1,0:T(1,128)} %slot_ref.5) | copy-start | bytes 100
  2.3 0.7 %copy-start.5 = (s32[2,1,8]{2,1,0:T(1,128)S(1)}, s32[2,1,8]{2,1,0:T(1,128)}, u32[]{:S(2)}) copy-start(s32[2,1,8]{2,1,0:T(1,128)} %corner_ref.2) | copy-start | bytes 196
  3.0 1.4 %copy-start.1 = (bf16[512,512]{1,0:T(8,128)(2,1)S(1)}, bf16[512,512]{1,0:T(8,128)(2,1)}, u32[]{:S(2)}) copy-start(bf16[512,512]{1,0:T(8,128)(2,1)} %b_ref.1) | copy-start | bytes 1572868
  4.5 18.3 %copy-start.2 = (s32[32,32]{1,0:T(8,128)S(1)}, s32[32,32]{1,0:T(8,128)}, u32[]{:S(2)}) copy-start(s32[32,32]{1,0:T(8,128)} %mask_ref.1) | copy-start | bytes 12292
  22.8 0.7 %copy-start.6 = (s32[2,1,8]{2,1,0:T(1,128)S(1)}, s32[2,1,8]{2,1,0:T(1,128)}, u32[]{:S(2)}) copy-start(s32[2,1,8]{2,1,0:T(1,128)} %corner_ref.3) | copy-start | bytes 196
  22.8 0.7 %copy-start.7 = (s32[1,8]{1,0:T(1,128)S(1)}, s32[1,8]{1,0:T(1,128)}, u32[]{:S(2)}) copy-start(s32[1,8]{1,0:T(1,128)} %slot_ref.4) | copy-start | bytes 100
  35.5 0.7 %copy-start.4 = (s32[1,8]{1,0:T(1,128)S(1)}, s32[1,8]{1,0:T(1,128)}, u32[]{:S(2)}) copy-start(s32[1,8]{1,0:T(1,128)} %slot_ref.5) | copy-start | bytes 100
where the time goes:
time: 48.2 us; the launch traced here: 48 us
  Pallas kernels  42.4 us (88%)
  local copies, waits for them, and re-layouts  4.87 us (10%)
  between operations  0.71 us (1%)
    pallas_call x1, Pallas kernels, gather(): pl.pallas_call(functools.partial(gather_kernel, n_ty, n_tx), out_shape=[j...  18.3 us
    pallas_call x1, Pallas kernels, pair_flows(): pl.pallas_call(functools.partial(flow_kernel, items, left_pad, tile), out...  12 us
    pallas_call x1, Pallas kernels, relax(): pl.pallas_call(functools.partial(relax_kernel, n_ty, n_tx), out_shape=[ja...  10.7 us
    unnamed x18, local copies, waits for them, and re-layouts  4.87 us
    pallas_call x1, Pallas kernels, cut_templates(): pl.pallas_call(functools.partial(cut_kernel, template_slot.shape[1]), out...  1.43 us

commit v1 on v0

--- a/solution.py
+++ b/solution.py
@@ -157,7 +157,7 @@
 
 
 def relax_kernel(
-    n_ty, n_tx, slot_ref, ret_ref, field_ref, owner_ref, moved_ref, landed, ext, send, recv, hsend, hrecv
+    n_ty, n_tx, table_ref, ret_ref, field_ref, owner_ref, moved_ref, landed, ext, send, recv, hsend, hrecv
 ):
     f32 = jnp.float32
     ty, tx = lax.axis_index("ty"), lax.axis_index("tx")
@@ -232,20 +232,20 @@
     for axis in range(2):
         out = jnp.zeros((1, LANES), f32)
         for j in range(items):
-            slot = slot_ref[0, j]
+            slot = table_ref[2, j]
             value = landed[slot // CAP, pl.ds(slot % CAP * 2 + axis, 1), :]
             out = jnp.where(out_lane == j, value, out)
         owner_ref[axis] = out[:, :items]
 
 
-def relax(template_slot, returned, field, cols, n_ty, n_tx):
+def relax(table, returned, field, cols, n_ty, n_tx):
     f32 = jnp.float32
     rows = field.shape[0]
     dma = pltpu.SemaphoreType.DMA
     return pl.pallas_call(
         functools.partial(relax_kernel, n_ty, n_tx),
         out_shape=[
-            jax.ShapeDtypeStruct((2, 1, template_slot.shape[1]), f32),
+            jax.ShapeDtypeStruct((2, 1, table.shape[1]), f32),
             jax.ShapeDtypeStruct((2, rows, cols), f32),
         ],
         in_specs=[SMEM, VMEM, VMEM],
@@ -262,46 +262,45 @@
             collective_id=1, has_side_effects=True, vmem_limit_bytes=8 * 2**20
         ),
         name="relax",
-    )(template_slot, returned, field)
-
-
-def cut_kernel(items, corner_ref, slot_ref, a_ref, out_ref, wide):
+    )(table, returned, field)
+
+
+def cut_kernel(items, table_ref, a_ref, out_ref, wide):
     rows, cols = a_ref.shape
     for part in range(cols // LANES):
         wide[part] = a_ref[:, part * LANES : (part + 1) * LANES].astype(jnp.float32)
     wide[cols // LANES] = jnp.zeros((rows, LANES), jnp.float32)
 
     def one(j, carry):
-        top = corner_ref[0, 0, j]
-        left = corner_ref[1, 0, j]
+        top = table_ref[0, j]
+        left = table_ref[1, j]
         base = left // LANES
         block = jnp.concatenate([wide[base + p, pl.ds(top, PATCH), :] for p in range(2)], axis=1)
         block = pltpu.roll(block, (2 * LANES - left % LANES) % (2 * LANES), 1)
-        out_ref[slot_ref[0, j]] = block[:, :PATCH].astype(jnp.bfloat16)
+        out_ref[table_ref[2, j]] = block[:, :PATCH].astype(jnp.bfloat16)
         return carry
 
     lax.fori_loop(0, items, one, 0)
 
 
-def cut_templates(section_a, template_corner, template_slot, slots):
+def cut_templates(section_a, table, slots):
     rows, cols = section_a.shape
     return pl.pallas_call(
-        functools.partial(cut_kernel, template_slot.shape[1]),
+        functools.partial(cut_kernel, table.shape[1]),
         out_shape=jax.ShapeDtypeStruct((slots, PATCH, PATCH), jnp.bfloat16),
-        in_specs=[SMEM, SMEM, VMEM],
+        in_specs=[SMEM, VMEM],
         out_specs=VMEM,
         scratch_shapes=[pltpu.VMEM((cols // LANES + 1, rows, LANES), jnp.float32)],
         compiler_params=pltpu.CompilerParams(vmem_limit_bytes=24 * 2**20),
         name="cut",
-    )(template_corner, template_slot, section_a)
+    )(table, section_a)
 
 
 def flow_kernel(
     items,
     left_pad,
     tile,
-    corner_ref,
-    slot_ref,
+    table_ref,
     b_ref,
     t_ref,
     mask_ref,
@@ -332,14 +331,14 @@
     win_lane = lax.broadcasted_iota(jnp.int32, (WIN, 2 * LANES), 1)
 
     def one(m, carry):
-        top = corner_ref[0, 0, m]
-        left = corner_ref[1, 0, m] + left_pad
+        top = table_ref[3, m]
+        left = table_ref[4, m] + left_pad
         base = left // LANES
         block = jnp.concatenate([wide[base + p, pl.ds(top, WIN), :] for p in range(3)], axis=1)
         block = pltpu.roll(block, (3 * LANES - left % LANES) % (3 * LANES), 1)
         window = jnp.where(win_lane < WIN, block[:, : 2 * LANES], 0.0)
         win[m, :WIN, :] = window
-        template = t_ref[slot_ref[0, m]]
+        template = t_ref[table_ref[5, m]]
         temp[m] = template.astype(f32)
         for s in range(16 // GROUP):
             shifted[m, s] = win[m, pl.ds(s * GROUP, shifted.shape[2]), :].astype(jnp.bfloat16)
@@ -417,11 +416,11 @@
     out_y = jnp.zeros((1, LANES), f32)
     out_x = jnp.zeros((1, LANES), f32)
     for m in range(items):
-        slot = slot_ref[0, m]
+        slot = table_ref[5, m]
         ret_ref[slot // CAP, pl.ds(slot % CAP * 2, 1), :] = flow_y[m]
         ret_ref[slot // CAP, pl.ds(slot % CAP * 2 + 1, 1), :] = flow_x[m]
-        centre_y = (corner_ref[0, 0, m] + PATCH // 2) * node_rows // tile
-        centre_x = (corner_ref[1, 0, m] + PATCH // 2) * node_cols // tile
+        centre_y = (table_ref[3, m] + PATCH // 2) * node_rows // tile
+        centre_x = (table_ref[4, m] + PATCH // 2) * node_cols // tile
         here = at_row == centre_y
         for part, value in ((1, -flow_y[m]), (2, -flow_x[m]), (3, 1.0)):
             at = at_col == centre_x + part * node_cols
@@ -434,8 +433,8 @@
     source_ref[1] = out_x[:, :items]
 
 
-def pair_flows(wide_b, arrived, window_corner, window_slot, node_mask, left_pad, tile, devices):
-    items = window_slot.shape[1]
+def pair_flows(wide_b, arrived, table, node_mask, left_pad, tile, devices):
+    items = table.shape[1]
     rows_b = wide_b.shape[0]
     node_rows = node_mask.shape[0]
     f32 = jnp.float32
@@ -448,7 +447,7 @@
             jax.ShapeDtypeStruct((node_rows, LANES), f32),
             jax.ShapeDtypeStruct((2, 1, items), f32),
         ],
-        in_specs=[SMEM, SMEM, VMEM, VMEM, VMEM],
+        in_specs=[SMEM, VMEM, VMEM, VMEM],
         out_specs=[VMEM, VMEM, VMEM],
         scratch_shapes=[
             pltpu.VMEM((cols_w // LANES, rows_b, LANES), f32),
@@ -460,7 +459,7 @@
         ],
         compiler_params=pltpu.CompilerParams(vmem_limit_bytes=32 * 2**20),
         name="pair_flows",
-    )(window_corner, window_slot, wide_b, arrived, node_mask)
+    )(table, wide_b, arrived, node_mask)
 
 
 def shards(
@@ -468,13 +467,16 @@
 ):
     tile = section_a.shape[0]
     n_ty, n_tx = lax.axis_size("ty"), lax.axis_size("tx")
-    outgoing = cut_templates(section_a, template_corner, template_slot, n_tx * CAP)
+    table = jnp.concatenate(
+        [template_corner[:, 0], template_slot, window_corner[:, 0], window_slot], axis=0
+    )
+    outgoing = cut_templates(section_a, table, n_tx * CAP)
     b_wide, arrived = gather(section_b, outgoing, n_ty, n_tx)
     returned, field, source_flow = pair_flows(
-        b_wide, arrived, window_corner, window_slot, node_mask, LANES - RADIUS, tile, n_tx
+        b_wide, arrived, table, node_mask, LANES - RADIUS, tile, n_tx
     )
     owner_flow, displace = relax(
-        template_slot, returned, field, node_mask.shape[1], n_ty, n_tx
+        table, returned, field, node_mask.shape[1], n_ty, n_tx
     )
     return (owner_flow, source_flow, displace)
 

time: 48.2 us -> 46.4 us (0.963)
  local copies, waits for them, and re-layouts: 4.87 us -> 2.91 us
    unnamed x18 -> x16, local copies, waits for them, and re-layouts: 4.87 us -> 2.91 us
where the time goes in v1:
time: 46.4 us; the launch traced here: 46.2 us
  Pallas kernels  42.6 us (92%)
  local copies, waits for them, and re-layouts  2.91 us (6%)
  between operations  0.72 us (2%)
    pallas_call x1, Pallas kernels, gather(): pl.pallas_call(functools.partial(gather_kernel, n_ty, n_tx), out_shape=[j...  18.3 us
    pallas_call x1, Pallas kernels, pair_flows(): pl.pallas_call(functools.partial(flow_kernel, items, left_pad, tile), out...  12.1 us
    pallas_call x1, Pallas kernels, relax(): pl.pallas_call(functools.partial(relax_kernel, n_ty, n_tx), out_shape=[ja...  10.8 us
    unnamed x16, local copies, waits for them, and re-layouts  2.91 us
    pallas_call x1, Pallas kernels, cut_templates(): pl.pallas_call(functools.partial(cut_kernel, table.shape[1]), out_shape=j...  1.48 us

profile of v1, /device:TPU:0, one launch (start us, length us, event | category | flops | bytes accessed | tf_op | source)
XLA Modules:
  0.0 46.2 jit_solution(5456068795507390659)
XLA Ops:
  0.6 0.0 copy-start.4
  0.6 0.0 copy-start.6
  0.7 0.0 copy-start.3
  0.7 0.0 copy-start.5
  0.7 0.6 %copy-done.4 = s32[2,1,8]{2,1,0:T(1,128)S(1)} copy-done((s32[2,1,8]{2,1,0:T(1,128)S(1)}, s32[2,1,8]{2,1,0:T(1,128)}, u32[]{:S(2)}) %copy-start.4) | copy-done | bytes 88
  1.3 0.0 copy-done.6
  1.3 0.0 copy-done.3
  1.3 0.0 copy-done.5
  1.4 0.0 copy-start
  1.4 1.0 %copy-done = bf16[512,512]{1,0:T(8,128)(2,1)S(1)} copy-done((bf16[512,512]{1,0:T(8,128)(2,1)S(1)}, bf16[512,512]{1,0:T(8,128)(2,1)}, u32[]{:S(2)}) %copy-start) | copy-done | bytes 524312
  2.4 0.0 copy-start.1
  2.4 1.5 %cut.1.out_ref = bf16[16,128,128]{2,1,0:T(8,128)(2,1)S(1)} custom-call(s32[6,8]{1,0:T(8,128)S(1)} %pad_add_fusion.table_ref, bf16[512,512]{1,0:T(8,128)(2,1)S(1)} %copy-done), custom_call_target="tpu_custom_call" | custom-call | tf_op jit(solution)/shard_map/cut/pallas_call | solution.py:288
  3.9 0.0 copy-done.1
  3.9 0.0 copy-start.2
  3.9 18.3 %gather.1 = (bf16[576,768]{1,0:T(8,128)(2,1)S(1)}, bf16[16,128,128]{2,1,0:T(8,128)(2,1)S(1)}) custom-call(bf16[512,512]{1,0:T(8,128)(2,1)S(1)} %copy-done.1, bf16[16,128,128]{2,1,0:T(8,128)(2,1)S(1)} %cut.1.out_ref), custom_call_target="tpu_custom_call" | custom-call | tf_op jit(solution)/shard_map/gather/pallas_call | solution.py:136
  22.2 0.0 copy-done.2
  22.2 12.1 %pair_flows.1 = (f32[8,8,128]{2,1,0:T(8,128)S(1)}, f32[32,128]{1,0:T(8,128)S(1)}, f32[2,1,8]{2,1,0:T(1,128)}) custom-call(s32[6,8]{1,0:T(8,128)S(1)} %pad_add_fusion.table_ref, bf16[576,768]{1,0:T(8,128)(2,1)S(1)} %get-tuple-element.10.b_ref, bf16[16,128,128]{2,1,0:T(8,128)(2,1)S(1)} %get-tuple-element.11.t_ref, s32[32,32]{1,0:T(8,128)S(1)} %copy-done.2), custom_call_target="tpu_custom_call" | custom-call | tf_op jit(solution)/shard_map/pair_flows/pallas_call | solution.py:443
  34.3 10.8 %relax.1 = (f32[2,1,8]{2,1,0:T(1,128)S(1)}, f32[2,32,32]{2,1,0:T(8,128)S(1)}) custom-call(s32[6,8]{1,0:T(8,128)S(1)} %pad_add_fusion.table_ref, f32[8,8,128]{2,1,0:T(8,128)S(1)} %get-tuple-element.12.ret_ref, f32[32,128]{1,0:T(8,128)S(1)} %get-tuple-element.13.field_ref), custom_call_target="tpu_custom_call" | custom-call | tf_op jit(solution)/shard_map/relax/pallas_call | solution.py:245
  45.1 0.6 %copy.12 = f32[2,1,8]{2,1,0:T(1,128)} copy(f32[2,1,8]{2,1,0:T(1,128)S(1)} %get-tuple-element.20) | data formatting | bytes 128
  45.6 0.6 %copy.13 = f32[2,32,32]{2,1,0:T(8,128)} copy(f32[2,32,32]{2,1,0:T(8,128)S(1)} %get-tuple-element.22) | data formatting | bytes 16384
  (1 shorter events, 0.0 us)
Async XLA Ops:
  0.6 0.7 %copy-start.4 = (s32[2,1,8]{2,1,0:T(1,128)S(1)}, s32[2,1,8]{2,1,0:T(1,128)}, u32[]{:S(2)}) copy-start(s32[2,1,8]{2,1,0:T(1,128)} %param.9) | copy-start | bytes 196
  0.6 0.7 %copy-start.6 = (s32[1,8]{1,0:T(1,128)S(1)}, s32[1,8]{1,0:T(1,128)}, u32[]{:S(2)}) copy-start(s32[1,8]{1,0:T(1,128)} %param.10) | copy-start | bytes 100
  0.7 0.7 %copy-start.3 = (s32[2,1,8]{2,1,0:T(1,128)S(1)}, s32[2,1,8]{2,1,0:T(1,128)}, u32[]{:S(2)}) copy-start(s32[2,1,8]{2,1,0:T(1,128)} %param.11) | copy-start | bytes 196
  0.7 0.7 %copy-start.5 = (s32[1,8]{1,0:T(1,128)S(1)}, s32[1,8]{1,0:T(1,128)}, u32[]{:S(2)}) copy-start(s32[1,8]{1,0:T(1,128)} %param.12) | copy-start | bytes 100
  1.4 1.0 %copy-start = (bf16[512,512]{1,0:T(8,128)(2,1)S(1)}, bf16[512,512]{1,0:T(8,128)(2,1)}, u32[]{:S(2)}) copy-start(bf16[512,512]{1,0:T(8,128)(2,1)} %a_ref.1) | copy-start | bytes 1572868
  2.4 1.5 %copy-start.1 = (bf16[512,512]{1,0:T(8,128)(2,1)S(1)}, bf16[512,512]{1,0:T(8,128)(2,1)}, u32[]{:S(2)}) copy-start(bf16[512,512]{1,0:T(8,128)(2,1)} %b_ref.1) | copy-start | bytes 1572868
  3.9 18.3 %copy-start.2 = (s32[32,32]{1,0:T(8,128)S(1)}, s32[32,32]{1,0:T(8,128)}, u32[]{:S(2)}) copy-start(s32[32,32]{1,0:T(8,128)} %mask_ref.1) | copy-start | bytes 12292
